TPU v7x, 1024 devices: a whole 4x8x16 slice. The times are simulated.
1024 devices in a mesh: dp: 64 (over y, x, core), tensor: 16 (over z).
Axes of the slice: x: 4, y: 8, z: 16, core: 2. Of those that a mesh axis runs over, the one named last changes fastest.
Arguments:
- patches: bfloat16 [32768, 1280], P('dp'), may hold values from -6 to 6
- live_blocks: int32 [64], P('dp'), may hold values from 1 to 4, as said below
- owner_map: int32 [8192, 1], P('dp'), may hold values from 0 to 63; in each aligned block of 128 rows (0 to 127, 128 to 255, ...) at most 2 rows name the same one
- vit_gain: float32 [1280], replicated, may hold values from 0.1 to 1.9
- fc1_weight: bfloat16 [1280, 5120], P(None, 'tensor'), may hold values from -0.15625 to 0.15625
- fc2_weight: bfloat16 [5120, 1280], P('tensor'), may hold values from -0.078125 to 0.078125
- merge_gain: float32 [1280], replicated, may hold values from 0.1 to 1.9
- mid_weight: bfloat16 [5120, 5120], P(None, 'tensor'), may hold values from -0.078125 to 0.078125
- proj_weight: bfloat16 [5120, 4096], P('tensor'), may hold values from -0.125 to 0.125
Outputs:
- llm_embeds: bfloat16 [8192, 4096], P('dp', 'tensor')
Inputs may be any that keep to these rules, and one draw needn't show every extreme that they name: `live_blocks`: each rank holds at least one live block; ranks 0, 31, 32 and 63 hold 4, and some rank between 1 and 30 holds one. `owner_map`: among the 128 rows of one rank no owner is named more than 2 times, and some owner exactly that often.
All inputs are finite; a program needn't handle non-finite values.
Results may differ from a plain program's by a relative error of at most 0.0095.
Values may be sent and summed in bfloat16 or wider, within the bound.
A program may use at most 64 MiB of HBM per device.

v0:
```python
import jax
import jax.numpy as jnp
from jax import lax
from jax.sharding import PartitionSpec as P

SLOTS = 4


def passed_along(value, axis, steps):
    count = lax.axis_size(axis)
    pairs = [(source, (source + steps) % count) for source in range(count)]
    return lax.ppermute(value, axis, pairs)


def layer_norm(values, gain):
    mean = jnp.mean(values, axis=-1, keepdims=True)
    centered = values - mean
    variance = jnp.mean(centered * centered, axis=-1, keepdims=True)
    return centered * lax.rsqrt(variance + 1e-06) * gain


def block_partials(work, flags, vit_gain, fc1_weight, fc2_weight):
    width = work.shape[1]
    blocks = work.reshape(SLOTS, work.shape[0] // SLOTS, width)

    def compute(rows):
        normed = layer_norm(rows.astype(jnp.float32), vit_gain).astype(jnp.bfloat16)
        up_vals = jnp.dot(normed, fc1_weight, preferred_element_type=jnp.float32)
        hidden = (up_vals * jax.nn.sigmoid(1.702 * up_vals)).astype(jnp.bfloat16)
        return jnp.dot(hidden, fc2_weight, preferred_element_type=jnp.float32)

    def vacant(rows):
        return jnp.zeros(rows.shape, jnp.float32)

    def one_block(items):
        rows, flag = items
        return lax.cond(flag, compute, vacant, rows)

    return lax.map(one_block, (blocks, flags)).reshape(work.shape[0], width)


def body(
    patches,
    live_blocks,
    owner_map,
    vit_gain,
    fc1_weight,
    fc2_weight,
    merge_gain,
    mid_weight,
    proj_weight,
):
    rows_all = patches.shape[0]
    width = patches.shape[1]
    blk = rows_all // SLOTS
    half = SLOTS // 2
    count = live_blocks[0]
    ndp = lax.axis_size("dp")
    slot_ids = jnp.arange(SLOTS, dtype=jnp.int32)
    incoming, partner_count = passed_along((patches[half * blk :], live_blocks), "dp", ndp // 2)
    work = jnp.concatenate([patches[: half * blk], incoming], axis=0)
    flags = jnp.where(slot_ids < half, slot_ids < count, slot_ids < partner_count[0])
    partials = block_partials(work, flags, vit_gain, fc1_weight, fc2_weight)
    merged_count = rows_all // 4
    partials = lax.psum(partials, "tensor")
    vit_out = (work.astype(jnp.float32) + partials).astype(jnp.bfloat16)
    merged = layer_norm(vit_out.astype(jnp.float32), merge_gain).astype(jnp.bfloat16)
    merged = merged.reshape(merged_count, 4 * width)
    lower = half * blk // 4
    returned = passed_along(merged[lower:], "dp", ndp // 2)
    merged = jnp.concatenate([merged[:lower], returned], axis=0)
    row_ids = jnp.arange(merged_count, dtype=jnp.int32)
    keep = row_ids * 4 // blk < count
    merged = jnp.where(keep[:, None], merged, jnp.zeros_like(merged))
    middle = jnp.dot(merged, mid_weight, preferred_element_type=jnp.float32)
    middle = jax.nn.gelu(middle, approximate=False).astype(jnp.bfloat16)
    capacity = (merged_count + ndp - 1) // ndp
    owners = owner_map[:, 0]
    same = (owners[:, None] == owners[None, :]) & (row_ids[None, :] < row_ids[:, None])
    slot = jnp.sum(same.astype(jnp.int32), axis=1)
    dest = owners * capacity + slot
    targets = jnp.arange(ndp * capacity, dtype=jnp.int32)
    placing = (targets[:, None] == dest[None, :]).astype(jnp.bfloat16)
    outgoing = jnp.dot(placing, middle, preferred_element_type=jnp.float32).astype(jnp.bfloat16)
    received = lax.all_to_all(outgoing, "dp", split_axis=0, concat_axis=0, tiled=True)
    terms = jnp.dot(received, proj_weight, preferred_element_type=jnp.float32)
    return lax.psum_scatter(terms, "tensor", scatter_dimension=1, tiled=True).astype(jnp.bfloat16)


def solution(mesh):
    placed = (
        P("dp", None),
        P("dp"),
        P("dp", None),
        P(),
        P(None, "tensor"),
        P("tensor", None),
        P(),
        P(None, "tensor"),
        P("tensor", None),
    )
    return jax.shard_map(
        body, mesh=mesh, in_specs=placed, out_specs=P("dp", "tensor"), check_vma=False
    )
```

profile of v0, /device:TPU:2, one launch (start us, length us, event | category | flops | bytes accessed | tf_op | source)
XLA Modules:
  0.0 382.5 jit_solution(5500954849424177427)
XLA Ops:
  6.5 0.0 copy-start
  6.5 0.0 all-reduce.2.cloned.1.call-start
  6.5 2.6 fusion.110
  9.2 0.0 copy-start.1
  9.2 7.9 %collective-permute-start = (bf16[256,1280]{1,0:T(8,128)(2,1)}, bf16[256,1280]{1,0:T(8,128)(2,1)}, u32[]{:S(2)}, u32[]{:S(2)}) collective-permute-start(bf16[256,1280]{1,0:T(8,128)(2,1)} %get-tuple-element.115), channel_id=1, source_target_pairs={{0,512},{16,528},{32,544},{48,560},{64,576},{80,592},{96,608},{112... | collective-permute-start | bytes 1966088 | tf_op jit(solution)/shard_map/ppermute | solution.py:12
  17.0 2.0 collective-permute-start.1
  19.7 2.2 copy.13
  21.9 23.5 %collective-permute-done.1 = s32[1]{0:T(128)} collective-permute-done((s32[1]{0:T(128)}, s32[1]{0:T(128)}, u32[]{:S(2)}, u32[]{:S(2)}) %collective-permute-start.1) | collective-permute-done | bytes 36 | tf_op jit(solution)/shard_map/ppermute | solution.py:12
  45.5 0.6 compare_select_fusion
  46.0 0.0 collective-permute-done
  46.0 2.5 pad_maximum_fusion
  48.5 0.0 copy-done.1
  48.5 21.7 %while.10 = (s32[]{:T(128)}, f32[4,128,1280]{2,1,0:T(8,128)}, pred[4]{0:T(512)(128)(4,1)S(1)}, bf16[4,128,1280]{2,1,0:T(8,128)(2,1)}, f32[1280]{0:T(1024)S(1)}, ...) while((s32[]{:T(128)}, f32[4,128,1280]{2,1,0:T(8,128)}, pred[4]{0:T(512)(128)(4,1)S(1)}, ...), condition=%wide.region_6.7_spmd, body=%wide.region_1.6_spmd.sunk | while | flops 211763328 | bytes 4762264 | solution.py:39
  48.5 0.7 dynamic_slice.22
  49.8 5.9 %conditional.2 = (f32[1,128,1280]{2,1,0:T(8,128)}) conditional(s32[]{:T(128)} %bitcast.34, () %tuple.36, (bf16[4,128,1280]{2,1,0:T(8,128)(2,1)}, s32[]{:T(128)}, f32[1280]{0:T(1024)S(1)}, bf16[1280,320]{1,0:T(8,128)(2,1)}, bf16[320,1280]{1,0:T(8,128)(2,1)}) %tuple.37), branch_computations={%region_2.2_spmd, %region_3.0_spmd} | conditional | flops 211763328 | bytes 3450896 | solution.py:37
  49.8 1.1 convert_reduce_fusion
  50.9 1.2 fusion.3
  52.1 3.6 convolution_bitcast_fusion
  55.7 2.0 constant_dynamic-update-slice_fusion.2
  57.7 0.7 dynamic_slice.22
  59.0 0.9 conditional.2
  59.0 0.9 broadcast_in_dim.16
  59.9 2.0 constant_dynamic-update-slice_fusion.2
  61.9 0.7 dynamic_slice.22
  63.2 0.9 conditional.2
  63.2 0.9 broadcast_in_dim.16
  64.1 2.0 constant_dynamic-update-slice_fusion.2
  66.0 0.7 dynamic_slice.22
  67.3 0.9 conditional.2
  67.3 0.9 broadcast_in_dim.16
  68.2 2.0 constant_dynamic-update-slice_fusion.2
  70.2 0.0 all-reduce.2.cloned.1.call-update
  70.2 0.0 copy-start.2
  70.2 0.0 reduce-scatter.2.cloned.1.call-start
  70.3 175.0 %all-reduce.2.cloned.1.call-done = f32[512,1280]{1,0:T(8,128)} async-done(((f32[512,1280]{1,0:T(8,128)}), f32[512,1280]{1,0:T(8,128)}) %all-reduce.2.cloned.1.call-update) | async-done | bytes 2621456 | tf_op jit(solution)/shard_map/psum | solution.py:65
  245.3 2.4 convert_reduce_fusion.1
  247.8 0.5 fusion.24
  248.3 0.0 copy-done.2
  248.3 0.5 fusion.26
  248.8 0.0 copy-start.3
  248.8 1.2 fusion.109
  249.9 2.3 slice.23
  252.2 7.2 %collective-permute-start.2 = (bf16[64,5120]{1,0:T(8,128)(2,1)}, bf16[64,5120]{1,0:T(8,128)(2,1)}, u32[]{:S(2)}, u32[]{:S(2)}) collective-permute-start(bf16[64,5120]{1,0:T(8,128)(2,1)} %slice.23), channel_id=1, source_target_pairs={{0,512},{16,528},{32,544},{48,560},{64,576},{80,592},{96,608},{112... | collective-permute-start | bytes 1966088 | tf_op jit(solution)/shard_map/ppermute | solution.py:12
  259.4 0.0 copy-done.3
  259.4 0.2 convert_reduce_fusion.2
  259.6 2.3 slice.21
  261.9 12.5 %collective-permute-done.2 = bf16[64,5120]{1,0:T(8,128)(2,1)} collective-permute-done((bf16[64,5120]{1,0:T(8,128)(2,1)}, bf16[64,5120]{1,0:T(8,128)(2,1)}, u32[]{:S(2)}, u32[]{:S(2)}) %collective-permute-start.2) | collective-permute-done | bytes 655392 | tf_op jit(solution)/shard_map/ppermute | solution.py:12
  274.4 0.0 copy-done
  274.4 2.9 convolution_convert_fusion
  277.3 0.1 copy.14
  277.4 0.1 all_to_all.8
  277.5 25.6 %all_to_all.12 = bf16[64,2,320]{2,1,0:T(2,128)(2,1)S(1)} all-to-all(bf16[64,2,320]{2,1,0:T(2,128)(2,1)S(1)} %all_to_all.8), channel_id=1, replica_groups=mesh['dp'=64,'tensor'=16] {'dp'}, dimensions={0} | all-to-all | bytes 163840 | tf_op jit(solution)/shard_map/all_to_all | solution.py:85
  303.1 0.1 all_to_all.10
  303.1 3.8 fusion.111
  307.0 0.0 reduce-scatter.2.cloned.1.call-update
  307.0 67.2 %reduce-scatter.2.cloned.1.call-done = f32[128,256]{1,0:T(8,128)} async-done(((f32[128,4096]{1,0:T(8,128)}), f32[128,256]{1,0:T(8,128)}) %reduce-scatter.2.cloned.1.call-update) | async-done | bytes 131088 | tf_op jit(solution)/shard_map/reduce_scatter | solution.py:87
  374.2 1.5 convert_element_type.53
  (7 shorter events, 0.1 us)
Async XLA Ops:
  6.5 267.9 %copy-start = (bf16[5120,320]{0,1:T(8,128)(2,1)S(1)}, bf16[5120,320]{0,1:T(8,128)(2,1)}, u32[]{:S(2)}) copy-start(bf16[5120,320]{0,1:T(8,128)(2,1)} %param.20) | copy-start | bytes 9830404
  6.5 238.8 %all-reduce.2.cloned.1.call-start = ((), (), s32[]{:S(2)}) async-start(), calls=%async_computation.2 | async-start | bytes 5242880 | tf_op jit(solution)/shard_map/psum | solution.py:65
  9.2 39.3 %copy-start.1 = (f32[1280]{0:T(1024)S(1)}, f32[1280]{0:T(1024)}, u32[]{:S(2)}) copy-start(f32[1280]{0:T(1024)} %param.16) | copy-start | bytes 15364
  9.2 36.9 %collective-permute-start = (bf16[256,1280]{1,0:T(8,128)(2,1)}, bf16[256,1280]{1,0:T(8,128)(2,1)}, u32[]{:S(2)}, u32[]{:S(2)}) collective-permute-start(bf16[256,1280]{1,0:T(8,128)(2,1)} %get-tuple-element.115), channel_id=1, source_target_pairs={{0,512},{16,528},{32,544},{48,560},{64,576},{80,592},{96,608},{112... | collective-permute-start | bytes 1966088 | tf_op jit(solution)/shard_map/ppermute | solution.py:12
  17.0 28.4 %collective-permute-start.1 = (s32[1]{0:T(128)}, s32[1]{0:T(128)}, u32[]{:S(2)}, u32[]{:S(2)}) collective-permute-start(s32[1]{0:T(128)} %param.14), channel_id=1, source_target_pairs={{0,512},{16,528},{32,544},{48,560},{64,576},{80,592},{96,608},{112... | collective-permute-start | bytes 20 | tf_op jit(solution)/shard_map/ppermute | solution.py:12
  70.2 178.0 %copy-start.2 = (f32[1280]{0:T(1024)S(1)}, f32[1280]{0:T(1024)}, u32[]{:S(2)}) copy-start(f32[1280]{0:T(1024)} %param.19) | copy-start | bytes 15364
  70.2 303.9 %reduce-scatter.2.cloned.1.call-start = ((), (), s32[]{:S(2)}) async-start(), calls=%async_computation.3 | async-start | bytes 2228224 | tf_op jit(solution)/shard_map/reduce_scatter | solution.py:87
  248.8 10.7 %copy-start.3 = (s32[128,1]{0,1:T(1,128)S(1)}, s32[128,1]{0,1:T(1,128)}, u32[]{:S(2)}) copy-start(s32[128,1]{0,1:T(1,128)} %param.15) | copy-start | bytes 1540
  252.2 22.2 %collective-permute-start.2 = (bf16[64,5120]{1,0:T(8,128)(2,1)}, bf16[64,5120]{1,0:T(8,128)(2,1)}, u32[]{:S(2)}, u32[]{:S(2)}) collective-permute-start(bf16[64,5120]{1,0:T(8,128)(2,1)} %slice.23), channel_id=1, source_target_pairs={{0,512},{16,528},{32,544},{48,560},{64,576},{80,592},{96,608},{112... | collective-permute-start | bytes 1966088 | tf_op jit(solution)/shard_map/ppermute | solution.py:12
Sparse Core Ops, SparseCore 0:
  70.4 174.9 all-reduce.1
  307.1 67.0 reduce-scatter.1
where the time goes:
time: 384 us; the launch traced here: 383 us
  waiting for transfers between devices  278 us (72%)
  blocking collectives  25.6 us (7%)
  local copies, waits for them, and re-layouts  24 us (6%)
  starting transfers between devices  17.1 us (4%)
  between operations  14.2 us (4%)
  other arithmetic  10.5 us (3%)
  matrix products  10.2 us (3%)
    psum x1, waiting for transfers between devices, body(): partials = lax.psum(partials, 'tensor')  175 us
    reduce_scatter x1, waiting for transfers between devices, body(): lax.psum_scatter(terms, 'tensor', scatter_dimension=1, tiled=True)  67.2 us
    ppermute x3, waiting for transfers between devices, passed_along(): return lax.ppermute(value, axis, pairs)  36 us
    all_to_all x1, blocking collectives, body(): lax.all_to_all(outgoing, 'dp', split_axis=0, concat_axis=0, tiled=True)  25.6 us
    ppermute x3, starting transfers between devices, passed_along(): return lax.ppermute(value, axis, pairs)  17.1 us
    dynamic_update_slice x4, local copies, waits for them, and re-layouts, block_partials(): return lax.map(one_block, (blocks, flags)).reshape(work.shape[0], width)  7.89 us
  transfers between devices with their start and end apart: 5, of which 4 were waited for; matrix products, arithmetic and copies ran while one was open for 1% of the time, Pallas kernels for 0%

commit v1 on v0

v1 whole, which is shorter than its diff:
```python
import jax
import jax.numpy as jnp
from jax import lax
from jax.experimental import pallas as pl
from jax.experimental.pallas import tpu as pltpu
from jax.sharding import PartitionSpec as P

MESH = pl.DeviceIdType.MESH
F32 = jnp.float32
BF16 = jnp.bfloat16
STAGES = 2
SIGNS = (1, -1)


def dot(a, b):
    return jnp.dot(a, b, preferred_element_type=F32)


def layer_norm(values, gain):
    mean = jnp.mean(values, axis=-1, keepdims=True)
    centered = values - mean
    variance = jnp.mean(centered * centered, axis=-1, keepdims=True)
    return centered * lax.rsqrt(variance + 1e-06) * gain


class Reduce:
    def __init__(self, me, ring, own, rounded, relay, got_far, got_near, send_sem, recv_sem):
        self.me, self.ring = me, ring
        self.own, self.rounded, self.relay = own, rounded, relay
        self.got_far, self.got_near = got_far, got_near
        self.send_sem, self.recv_sem = send_sem, recv_sem

    def place(self, steps):
        return lax.rem(self.me + (steps + self.ring), self.ring)

    def far(self, d, k, source=None):
        source = self.relay.at[d, k] if source is None else source
        return pltpu.make_async_remote_copy(
            src_ref=source, dst_ref=self.got_far.at[d, k],
            send_sem=self.send_sem.at[d, k, 0], recv_sem=self.recv_sem.at[d, k, 0],
            device_id={"tensor": self.place(2 * SIGNS[d])}, device_id_type=MESH)

    def near(self, d, k):
        return pltpu.make_async_remote_copy(
            src_ref=self.rounded.at[self.place((7 - 2 * k) * SIGNS[d])], dst_ref=self.got_near.at[d, k],
            send_sem=self.send_sem.at[d, k, 1], recv_sem=self.recv_sem.at[d, k, 1],
            device_id={"tensor": self.place(SIGNS[d])}, device_id_type=MESH)

    def first(self):
        self.far(0, 0, self.rounded.at[self.place(8)]).start()
        for d in (0, 1):
            self.near(d, 0).start()
        for d in (0, 1):
            self.near(d, 1).start()

    def arrived(self, d, k):
        if not (d == 1 and k == 0):
            self.far(d, k).wait_recv()
        self.near(d, k).wait_recv()
        total = self.got_near[d, k].astype(F32)
        if not (d == 1 and k == 0):
            total = total + self.got_far[d, k].astype(F32)
        return total

    def step(self, k):
        for d in (0, 1):
            got = self.arrived(d, k - 1)
            mine = self.own[self.place((8 - 2 * k) * SIGNS[d])]
            self.relay[d, k] = (mine + got).astype(BF16)
            self.far(d, k).start()
            if k < 3:
                self.near(d, k + 1).start()

    def last(self):
        return self.own[self.me] + self.arrived(0, 3) + self.arrived(1, 3)

    def drain(self):
        for d in (0, 1):
            for k in range(4):
                if not (d == 1 and k == 0):
                    self.far(d, k).wait_send()
                self.near(d, k).wait_send()


class Gather:
    def __init__(self, me, ring, chunks, send_sem, recv_sem):
        self.me, self.ring, self.chunks = me, ring, chunks
        self.send_sem, self.recv_sem = send_sem, recv_sem

    def place(self, steps):
        return lax.rem(self.me + (steps + self.ring), self.ring)

    def copy(self, d, k, near):
        chunk = self.chunks.at[self.place(-2 * k * SIGNS[d])]
        return pltpu.make_async_remote_copy(
            src_ref=chunk, dst_ref=chunk,
            send_sem=self.send_sem.at[d, k, near], recv_sem=self.recv_sem.at[d, k, near],
            device_id={"tensor": self.place((2 - near) * SIGNS[d])}, device_id_type=MESH)

    def landing(self, d, k, near):
        chunk = self.chunks.at[self.place((-2 * (k + 1) + near) * SIGNS[d])]
        return pltpu.make_async_remote_copy(
            src_ref=chunk, dst_ref=chunk,
            send_sem=self.send_sem.at[d, k, near], recv_sem=self.recv_sem.at[d, k, near],
            device_id={"tensor": self.place((2 - near) * SIGNS[d])}, device_id_type=MESH)

    def step(self, k):
        for d in (0, 1):
            if k > 0:
                self.landing(d, k - 1, 0).wait_recv()
            if not (d == 1 and k == 3):
                self.copy(d, k, 0).start()
        for d in (0, 1):
            self.copy(d, k, 1).start()

    def last(self):
        self.landing(0, 3, 0).wait_recv()
        for d in (0, 1):
            for k in range(4):
                self.landing(d, k, 1).wait_recv()

    def drain(self):
        for d in (0, 1):
            for k in range(4):
                if not (d == 1 and k == 3):
                    self.copy(d, k, 0).wait_send()
                self.copy(d, k, 1).wait_send()


def kernel(
    live_ref, owner_ref, vit_gain_ref, merge_gain_ref, patches_ref, fc1_ref, fc2_ref, mid_hbm, proj_hbm,
    out_ref,
    mid_w, proj_w, rows, own1, round1, relay1, far1, near1, chunks, own2, round2, relay2, far2, near2,
    outgoing, incoming,
    weight_sem, send1, recv1, send_g, recv_g, send2, recv2, send_x, recv_x,
):
    ring = lax.axis_size("tensor")
    ndp = lax.axis_size("dp")
    me = lax.axis_index("tensor")
    here = lax.axis_index("dp")
    merged = patches_ref.shape[0] // 4
    count = merged // STAGES
    width = patches_ref.shape[1]

    load_mid = pltpu.make_async_copy(mid_hbm, mid_w, weight_sem.at[0])
    load_proj = pltpu.make_async_copy(proj_hbm, proj_w, weight_sem.at[1])
    load_mid.start()
    load_proj.start()

    barrier = pltpu.get_barrier_semaphore()
    for hops in (1, 2, ring - 2, ring - 1):
        pl.semaphore_signal(barrier, inc=1, device_id={"tensor": lax.rem(me + hops, ring)}, device_id_type=MESH)

    def greet(hops, carry):
        pl.semaphore_signal(barrier, inc=1, device_id={"dp": lax.rem(here + hops, ndp)}, device_id_type=MESH)
        return carry

    lax.fori_loop(1, ndp, greet, 0)

    def mlp(s):
        total = 4 * count
        to = lax.broadcasted_iota(jnp.int32, (total, total), 0)
        source = lax.broadcasted_iota(jnp.int32, (total, total), 1)
        order = (source == 4 * (to % count) + to // count).astype(BF16)
        ordered = dot(order, patches_ref[s * total : (s + 1) * total, :])
        rows[s] = ordered.astype(BF16).reshape(rows.shape[1:])
        normed = layer_norm(ordered, vit_gain_ref[...]).astype(BF16)
        up = dot(normed, fc1_ref[...])
        hidden = (up * jax.nn.sigmoid(1.702 * up)).astype(BF16)
        partial = dot(hidden, fc2_ref[...]).reshape(rows.shape[1:])
        own1[s] = partial
        round1[s] = partial.astype(BF16)

    stages = range(STAGES)
    sums1 = [
        Reduce(me, ring, own1.at[s], round1.at[s], relay1.at[s], far1.at[s], near1.at[s], send1.at[s], recv1.at[s])
        for s in stages
    ]
    gathers = [Gather(me, ring, chunks.at[s], send_g.at[s], recv_g.at[s]) for s in stages]
    sums2 = [
        Reduce(me, ring, own2.at[s], round2.at[s], relay2.at[s], far2.at[s], near2.at[s], send2.at[s], recv2.at[s])
        for s in stages
    ]

    for s in stages:
        mlp(s)
        if s == 0:
            pl.semaphore_wait(barrier, 4 + ndp - 1)
        sums1[s].first()
    for k in (1, 2, 3):
        for s in stages:
            sums1[s].step(k)
    for s in stages:
        vit_out = (rows[s, me].astype(F32) + sums1[s].last()).astype(BF16)
        chunks[s, me] = layer_norm(vit_out.astype(F32), merge_gain_ref[...]).astype(BF16)
        gathers[s].step(0)
    for k in (1, 2, 3):
        for s in stages:
            gathers[s].step(k)
    load_mid.wait()
    load_proj.wait()
    emb = own2.shape[3]
    for s in stages:
        gathers[s].last()
        middle = jnp.zeros((count, mid_w.shape[1]), F32)
        part = ring // 4
        for j in range(4):
            block = chunks[s, part * j : part * (j + 1)].reshape(count, width)
            middle = middle + dot(block, mid_w[j * width : (j + 1) * width, :])
        middle = (0.5 * middle * (1.0 + lax.erf(middle * 0.7071067811865476))).astype(BF16)
        for t in range(ring):
            term = dot(middle, proj_w[:, t * emb : (t + 1) * emb])
            own2[s, t] = term
            round2[s, t] = term.astype(BF16)
        sums2[s].first()
    for k in (1, 2, 3):
        for s in stages:
            sums2[s].step(k)

    owner = jnp.broadcast_to(owner_ref[...].astype(F32), (merged, merged)).T.astype(jnp.int32)
    across = lax.broadcasted_iota(jnp.int32, (merged, merged), 1)
    down = lax.broadcasted_iota(jnp.int32, (merged, merged), 0)
    own_col = jnp.broadcast_to(owner_ref[...], (merged, merged))
    slot = jnp.sum(jnp.where((owner == own_col) & (down < across), 1.0, 0.0), axis=0, keepdims=True)
    column = lax.broadcasted_iota(jnp.int32, (ndp, merged), 1)
    target = lax.broadcasted_iota(jnp.int32, (ndp, merged), 0)
    kept = (owner[:1] == target) & (column * 4 // (4 * merged // 4) < live_ref[0])
    placing = [jnp.where(kept & (slot == float(k)), 1.0, 0.0).astype(BF16) for k in (0, 1)]

    final = jnp.concatenate([sums2[s].last().astype(BF16) for s in stages], axis=0)
    lanes = outgoing.shape[2]
    for k in (0, 1):
        placed = dot(placing[k], final)
        for h in range(emb // lanes):
            outgoing[:, 2 * k + h, :] = placed[:, h * lanes : (h + 1) * lanes]

    def send(hops, carry):
        peer = lax.rem(here + hops, ndp)
        pltpu.make_async_remote_copy(
            src_ref=outgoing.at[peer], dst_ref=incoming.at[here], send_sem=send_x, recv_sem=recv_x,
            device_id={"dp": peer}, device_id_type=MESH).start()
        return carry

    lax.fori_loop(1, ndp, send, 0)
    incoming[here] = outgoing[here]
    for s in stages:
        sums1[s].drain()
        gathers[s].drain()
        sums2[s].drain()
    others = pl.ds(0, ndp - 1)
    pltpu.make_async_copy(outgoing.at[others], incoming.at[others], send_x).wait()
    pltpu.make_async_copy(outgoing.at[others], incoming.at[others], recv_x).wait()

    row = lax.broadcasted_iota(jnp.int32, (2 * ndp, ndp), 0)
    origin = lax.broadcasted_iota(jnp.int32, (2 * ndp, ndp), 1)
    result = jnp.zeros((2 * ndp, emb), F32)
    for k in (0, 1):
        part = jnp.concatenate([incoming[:, 2 * k + h, :] for h in range(emb // lanes)], axis=1).astype(BF16)
        result = result + dot((row == 2 * origin + k).astype(BF16), part)
    out_ref[...] = result.astype(BF16)


def solution(mesh):
    ring, ndp = mesh.shape["tensor"], mesh.shape["dp"]

    def body(patches, live, owners, vit_gain, fc1, fc2, merge_gain, mid, proj):
        total, width = patches.shape
        chunk = total // STAGES // ring
        count = total // 4 // STAGES
        emb = proj.shape[1] // ring
        vmem = pl.BlockSpec(memory_space=pltpu.VMEM)
        return pl.pallas_call(
            kernel,
            out_shape=jax.ShapeDtypeStruct((2 * ndp, emb), BF16),
            in_specs=[pl.BlockSpec(memory_space=pltpu.SMEM)] + [vmem] * 6 + [pl.BlockSpec(memory_space=pl.ANY)] * 2,
            out_specs=vmem,
            scratch_shapes=[
                pltpu.VMEM(mid.shape, BF16),
                pltpu.VMEM(proj.shape, BF16),
                pltpu.VMEM((STAGES, ring, chunk, width), BF16),
                pltpu.VMEM((STAGES, ring, chunk, width), F32),
                pltpu.VMEM((STAGES, ring, chunk, width), BF16),
                pltpu.VMEM((STAGES, 2, 4, chunk, width), BF16),
                pltpu.VMEM((STAGES, 2, 4, chunk, width), BF16),
                pltpu.VMEM((STAGES, 2, 4, chunk, width), BF16),
                pltpu.VMEM((STAGES, ring, chunk, width), BF16),
                pltpu.VMEM((STAGES, ring, count, emb), F32),
                pltpu.VMEM((STAGES, ring, count, emb), BF16),
                pltpu.VMEM((STAGES, 2, 4, count, emb), BF16),
                pltpu.VMEM((STAGES, 2, 4, count, emb), BF16),
                pltpu.VMEM((STAGES, 2, 4, count, emb), BF16),
                pltpu.VMEM((ndp, 2 * emb // 128, 128), F32),
                pltpu.VMEM((ndp, 2 * emb // 128, 128), F32),
                pltpu.SemaphoreType.DMA((2,)),
            ]
            + [pltpu.SemaphoreType.DMA((STAGES, 2, 4, 2))] * 6
            + [pltpu.SemaphoreType.DMA, pltpu.SemaphoreType.DMA],
            compiler_params=pltpu.CompilerParams(
                collective_id=0, has_side_effects=True, vmem_limit_bytes=56 * 2**20
            ),
            name="vision_block",
        )(live, owners, vit_gain.reshape(1, width), merge_gain.reshape(1, width), patches, fc1, fc2, mid, proj)

    return jax.shard_map(
        body,
        mesh=mesh,
        in_specs=(
            P("dp", None), P("dp"), P("dp", None), P(), P(None, "tensor"), P("tensor", None), P(),
            P(None, "tensor"), P("tensor", None),
        ),
        out_specs=P("dp", "tensor"),
        check_vma=False,
    )
```

time: 384 us -> 115 us (0.30)
  the two profiles are of different devices: /device:TPU:2 before, /device:TPU:1 now
where the time goes in v1:
time: 115 us
  Pallas kernels  100 us (87%)
  local copies, waits for them, and re-layouts  13.5 us (12%)
    pallas_call x1, Pallas kernels, body(): pl.pallas_call(kernel, out_shape=jax.ShapeDtypeStruct((2 * ndp, emb), BF1...  100 us
    unnamed x4, local copies, waits for them, and re-layouts  10.9 us

profile of v1, /device:TPU:1, one launch (start us, length us, event | category | flops | bytes accessed | tf_op | source)
XLA Modules:
  0.0 114.5 jit_solution(6868353482332578181)
XLA Ops:
  0.7 1.3 %reshape.6.vit_gain_ref = f32[1,1280]{1,0:T(1,128)} reshape(f32[1280]{0:T(1024)} %param.12) | data formatting | bytes 10240 | tf_op jit(solution)/shard_map/reshape | solution.py:302
  1.9 1.3 %reshape.7.merge_gain_ref = f32[1,1280]{1,0:T(1,128)} reshape(f32[1280]{0:T(1024)} %param.15) | data formatting | bytes 10240 | tf_op jit(solution)/shard_map/reshape | solution.py:302
  3.2 1.4 %copy.10.owner_ref = s32[128,1]{1,0:T(8,128)} copy(s32[128,1]{0,1:T(1,128)} %param.11) | data formatting | bytes 1024 | tf_op args[2]
  4.6 2.2 %copy.11.fc1_ref = bf16[1280,320]{1,0:T(8,128)(2,1)} copy(bf16[1280,320]{0,1:T(8,128)(2,1)} %param.13) | data formatting | bytes 1638400 | tf_op args[4]
  6.8 5.8 %copy.12.mid_hbm = bf16[5120,320]{1,0:T(8,128)(2,1)} copy(bf16[5120,320]{0,1:T(8,128)(2,1)} %param.16) | data formatting | bytes 6553600 | tf_op args[7]
  12.7 100.4 %vision_block.1 = bf16[128,256]{1,0:T(8,128)(2,1)} custom-call(s32[1]{0:T(128)S(6)} %copy.14.live_ref, s32[128,1]{1,0:T(8,128)} %copy.10.owner_ref, f32[1,1280]{1,0:T(1,128)} %reshape.6.vit_gain_ref, f32[1,1280]{1,0:T(1,128)} %reshape.7.merge_gain_ref, bf16[512,1280]{1,0:T(8,128)(2,1)} %patches_ref.1, bf16[1280,320]{1,0:T(8,128)(2,1)} %copy.11.fc1_ref, ...), custom_call_target="tpu_custom_call" | custom-call | tf_op jit(solution)/shard_map/vision_block/pallas_call | solution.py:272
  113.1 1.5 %copy.15 = bf16[128,256]{1,0:T(8,128)(2,1)} copy(bf16[128,256]{1,0:T(8,128)(2,1)} %vision_block.1) | data formatting | bytes 131072

commit v2 on v1

v2 whole, which is shorter than its diff:
```python
import jax
import jax.numpy as jnp
from jax import lax
from jax.experimental import pallas as pl
from jax.experimental.pallas import tpu as pltpu
from jax.sharding import PartitionSpec as P

MESH = pl.DeviceIdType.MESH
F32 = jnp.float32
BF16 = jnp.bfloat16
STAGES = 2
HALVES = 2
SIGNS = (1, -1)


def dot(a, b):
    return jnp.dot(a, b, preferred_element_type=F32)


def dot_t(a, b):
    return lax.dot_general(a, b, (((1,), (1,)), ((), ())), preferred_element_type=F32)


def layer_norm(values, gain):
    mean = jnp.mean(values, axis=-1, keepdims=True)
    centered = values - mean
    variance = jnp.mean(centered * centered, axis=-1, keepdims=True)
    return centered * lax.rsqrt(variance + 1e-06) * gain


class Reduce:
    def __init__(self, me, ring, longer, own, rounded, relay, got_far, got_near, send_sem, recv_sem):
        self.me, self.ring, self.longer = me, ring, longer
        self.own, self.rounded, self.relay = own, rounded, relay
        self.got_far, self.got_near = got_far, got_near
        self.send_sem, self.recv_sem = send_sem, recv_sem

    def place(self, steps):
        return lax.rem(self.me + (steps + self.ring), self.ring)

    def far(self, d, k, source=None):
        source = self.relay.at[d, k] if source is None else source
        return pltpu.make_async_remote_copy(
            src_ref=source, dst_ref=self.got_far.at[d, k],
            send_sem=self.send_sem.at[d, k, 0], recv_sem=self.recv_sem.at[d, k, 0],
            device_id={"tensor": self.place(2 * SIGNS[d])}, device_id_type=MESH)

    def near(self, d, k):
        return pltpu.make_async_remote_copy(
            src_ref=self.rounded.at[self.place((7 - 2 * k) * SIGNS[d])], dst_ref=self.got_near.at[d, k],
            send_sem=self.send_sem.at[d, k, 1], recv_sem=self.recv_sem.at[d, k, 1],
            device_id={"tensor": self.place(SIGNS[d])}, device_id_type=MESH)

    def first(self):
        self.far(self.longer, 0, self.rounded.at[self.place(8)]).start()
        for d in (0, 1):
            self.near(d, 0).start()
        for d in (0, 1):
            self.near(d, 1).start()

    def arrived(self, d, k):
        if k > 0 or d == self.longer:
            self.far(d, k).wait_recv()
        self.near(d, k).wait_recv()
        total = self.got_near[d, k].astype(F32)
        if k > 0 or d == self.longer:
            total = total + self.got_far[d, k].astype(F32)
        return total

    def step(self, k):
        for d in (0, 1):
            got = self.arrived(d, k - 1)
            mine = self.own[self.place((8 - 2 * k) * SIGNS[d])]
            self.relay[d, k] = (mine + got).astype(BF16)
            self.far(d, k).start()
            if k < 3:
                self.near(d, k + 1).start()

    def last(self):
        return self.own[self.me] + self.arrived(0, 3) + self.arrived(1, 3)

    def drain(self):
        for d in (0, 1):
            for k in range(4):
                if k > 0 or d == self.longer:
                    self.far(d, k).wait_send()
                self.near(d, k).wait_send()


class Gather:
    def __init__(self, me, ring, longer, chunks, send_sem, recv_sem):
        self.me, self.ring, self.longer, self.chunks = me, ring, longer, chunks
        self.send_sem, self.recv_sem = send_sem, recv_sem

    def place(self, steps):
        return lax.rem(self.me + (steps + self.ring), self.ring)

    def copy(self, d, k, near):
        chunk = self.chunks.at[self.place(-2 * k * SIGNS[d])]
        return pltpu.make_async_remote_copy(
            src_ref=chunk, dst_ref=chunk,
            send_sem=self.send_sem.at[d, k, near], recv_sem=self.recv_sem.at[d, k, near],
            device_id={"tensor": self.place((2 - near) * SIGNS[d])}, device_id_type=MESH)

    def landing(self, d, k, near):
        chunk = self.chunks.at[self.place((-2 * (k + 1) + near) * SIGNS[d])]
        return pltpu.make_async_remote_copy(
            src_ref=chunk, dst_ref=chunk,
            send_sem=self.send_sem.at[d, k, near], recv_sem=self.recv_sem.at[d, k, near],
            device_id={"tensor": self.place((2 - near) * SIGNS[d])}, device_id_type=MESH)

    def step(self, k):
        for d in (0, 1):
            if k > 0:
                self.landing(d, k - 1, 0).wait_recv()
            if k < 3 or d == self.longer:
                self.copy(d, k, 0).start()
        for d in (0, 1):
            self.copy(d, k, 1).start()

    def last(self):
        self.landing(self.longer, 3, 0).wait_recv()
        for d in (0, 1):
            for k in range(4):
                self.landing(d, k, 1).wait_recv()

    def drain(self):
        for d in (0, 1):
            for k in range(4):
                if k < 3 or d == self.longer:
                    self.copy(d, k, 0).wait_send()
                self.copy(d, k, 1).wait_send()


def kernel(
    live_ref, owner_ref, vit_gain_ref, merge_gain_ref, patches_hbm, fc1_hbm, fc2_hbm, mid_hbm, proj_hbm,
    out_ref,
    patches_ref, fc1_ref, fc2_ref, mid_w, proj_w,
    rows, own1, round1, relay1, far1, near1, chunks, own2, round2, relay2, far2, near2,
    outgoing, incoming,
    load_sem, send1, recv1, send_g, recv_g, send2, recv2, send_x, recv_x,
):
    ring = lax.axis_size("tensor")
    ndp = lax.axis_size("dp")
    me = lax.axis_index("tensor")
    here = lax.axis_index("dp")
    merged = patches_ref.shape[0] // 4
    count = merged // STAGES
    width = patches_ref.shape[1]
    part = width // HALVES
    emb = own2.shape[4]

    barrier = pltpu.get_barrier_semaphore()
    for hops in (1, 2, ring - 2, ring - 1):
        pl.semaphore_signal(barrier, inc=1, device_id={"tensor": lax.rem(me + hops, ring)}, device_id_type=MESH)
    loads = [
        pltpu.make_async_copy(source, target, load_sem.at[i])
        for i, (source, target) in enumerate((
            (patches_hbm, patches_ref), (fc1_hbm, fc1_ref), (fc2_hbm, fc2_ref), (mid_hbm, mid_w), (proj_hbm, proj_w)))
    ]
    for load in loads:
        load.start()

    def greet(hops, carry):
        pl.semaphore_signal(barrier, inc=1, device_id={"dp": lax.rem(here + hops, ndp)}, device_id_type=MESH)
        return carry

    lax.fori_loop(1, ndp, greet, 0)

    def mlp(s):
        total = 4 * count
        to = lax.broadcasted_iota(jnp.int32, (total, total), 0)
        source = lax.broadcasted_iota(jnp.int32, (total, total), 1)
        order = (source == 4 * (to % count) + to // count).astype(BF16)
        ordered = dot(order, patches_ref[s * total : (s + 1) * total, :])
        rows[s] = ordered.astype(BF16).reshape(rows.shape[1:])
        normed = layer_norm(ordered, vit_gain_ref[...].reshape(1, width)).astype(BF16)
        up = dot_t(normed, fc1_ref[...])
        hidden = (up * jax.nn.sigmoid(1.702 * up)).astype(BF16)
        for h in range(HALVES):
            partial = dot(hidden, fc2_ref[:, h * part : (h + 1) * part]).reshape(own1.shape[2:])
            own1[s, h] = partial
            round1[s, h] = partial.astype(BF16)

    stages, halves = range(STAGES), range(HALVES)
    chains = [(s, h) for s in stages for h in halves]
    sums1 = {
        c: Reduce(me, ring, c[1], own1.at[c], round1.at[c], relay1.at[c], far1.at[c], near1.at[c], send1.at[c], recv1.at[c])
        for c in chains
    }
    gathers = {c: Gather(me, ring, c[1], chunks.at[c], send_g.at[c], recv_g.at[c]) for c in chains}
    sums2 = {
        c: Reduce(me, ring, c[1], own2.at[c], round2.at[c], relay2.at[c], far2.at[c], near2.at[c], send2.at[c], recv2.at[c])
        for c in chains
    }

    for load in loads[:3]:
        load.wait()
    for s in stages:
        mlp(s)
        if s == 0:
            pl.semaphore_wait(barrier, 4 + ndp - 1)
        for h in halves:
            sums1[s, h].first()
    for k in (1, 2, 3):
        for c in chains:
            sums1[c].step(k)
    for s in stages:
        summed = jnp.concatenate([sums1[s, h].last() for h in halves], axis=1)
        vit_out = (rows[s, me].astype(F32) + summed).astype(BF16)
        normed = layer_norm(vit_out.astype(F32), merge_gain_ref[...].reshape(1, width)).astype(BF16)
        for h in halves:
            chunks[s, h, me] = normed[:, h * part : (h + 1) * part]
            gathers[s, h].step(0)
    for k in (1, 2, 3):
        for c in chains:
            gathers[c].step(k)
    for load in loads[3:]:
        load.wait()
    quarter = ring // 4
    for s in stages:
        middle = jnp.zeros((count, mid_w.shape[0]), F32)
        for h in halves:
            gathers[s, h].last()
            for j in range(4):
                block = chunks[s, h, quarter * j : quarter * (j + 1)].reshape(count, part)
                first = j * width + h * part
                middle = middle + dot_t(block, mid_w[:, first : first + part])
        middle = (0.5 * middle * (1.0 + lax.erf(middle * 0.7071067811865476))).astype(BF16)
        for t in range(ring):
            term = dot(middle, proj_w[:, t * emb : (t + 1) * emb])
            for h in halves:
                piece = term[h * (count // HALVES) : (h + 1) * (count // HALVES)]
                own2[s, h, t] = piece
                round2[s, h, t] = piece.astype(BF16)
        for h in halves:
            sums2[s, h].first()
    for k in (1, 2, 3):
        for c in chains:
            sums2[c].step(k)

    owner = jnp.broadcast_to(owner_ref[...], (merged, merged))
    across = lax.broadcasted_iota(jnp.int32, (merged, merged), 1)
    down = lax.broadcasted_iota(jnp.int32, (merged, merged), 0)
    own_col = owner.astype(F32).T.astype(jnp.int32)
    slot = jnp.sum(jnp.where((owner == own_col) & (down < across), 1.0, 0.0), axis=0, keepdims=True)
    column = lax.broadcasted_iota(jnp.int32, (ndp, merged), 1)
    target = lax.broadcasted_iota(jnp.int32, (ndp, merged), 0)
    kept = (owner[:1] == target) & (column * 4 // (4 * merged // 4) < live_ref[0])
    placing = [jnp.where(kept & (slot == float(k)), 1.0, 0.0).astype(BF16) for k in (0, 1)]

    final = jnp.concatenate([sums2[c].last().astype(BF16) for c in chains], axis=0)
    lanes = outgoing.shape[2]
    for k in (0, 1):
        placed = dot(placing[k], final)
        for h in range(emb // lanes):
            outgoing[:, 2 * k + h, :] = placed[:, h * lanes : (h + 1) * lanes]

    def send(hops, carry):
        peer = lax.rem(here + hops, ndp)
        pltpu.make_async_remote_copy(
            src_ref=outgoing.at[peer], dst_ref=incoming.at[here], send_sem=send_x, recv_sem=recv_x,
            device_id={"dp": peer}, device_id_type=MESH).start()
        return carry

    lax.fori_loop(1, ndp, send, 0)
    incoming[here] = outgoing[here]
    for c in chains:
        sums1[c].drain()
        gathers[c].drain()
        sums2[c].drain()
    others = pl.ds(0, ndp - 1)
    pltpu.make_async_copy(outgoing.at[others], incoming.at[others], send_x).wait()
    pltpu.make_async_copy(outgoing.at[others], incoming.at[others], recv_x).wait()

    row = lax.broadcasted_iota(jnp.int32, (2 * ndp, ndp), 0)
    origin = lax.broadcasted_iota(jnp.int32, (2 * ndp, ndp), 1)
    result = jnp.zeros((2 * ndp, emb), F32)
    for k in (0, 1):
        part = jnp.concatenate([incoming[:, 2 * k + h, :] for h in range(emb // lanes)], axis=1).astype(BF16)
        result = result + dot((row == 2 * origin + k).astype(BF16), part)
    out_ref[...] = result.astype(BF16)


def solution(mesh):
    ring, ndp = mesh.shape["tensor"], mesh.shape["dp"]

    def body(patches, live, owners, vit_gain, fc1, fc2, merge_gain, mid, proj):
        total, width = patches.shape
        chunk = total // STAGES // ring
        count = total // 4 // STAGES
        emb = proj.shape[1] // ring
        vmem = pl.BlockSpec(memory_space=pltpu.VMEM)
        part, rows = width // HALVES, count // HALVES
        lead = (STAGES, HALVES)
        return pl.pallas_call(
            kernel,
            out_shape=jax.ShapeDtypeStruct((2 * ndp, emb), BF16),
            in_specs=[pl.BlockSpec(memory_space=pltpu.SMEM)] + [vmem] * 3 + [pl.BlockSpec(memory_space=pl.ANY)] * 5,
            out_specs=vmem,
            scratch_shapes=[
                pltpu.VMEM(patches.shape, BF16),
                pltpu.VMEM(fc1.shape[::-1], BF16),
                pltpu.VMEM(fc2.shape, BF16),
                pltpu.VMEM(mid.shape[::-1], BF16),
                pltpu.VMEM(proj.shape, BF16),
                pltpu.VMEM((STAGES, ring, chunk, width), BF16),
                pltpu.VMEM(lead + (ring, chunk, part), F32),
                pltpu.VMEM(lead + (ring, chunk, part), BF16),
                pltpu.VMEM(lead + (2, 4, chunk, part), BF16),
                pltpu.VMEM(lead + (2, 4, chunk, part), BF16),
                pltpu.VMEM(lead + (2, 4, chunk, part), BF16),
                pltpu.VMEM(lead + (ring, chunk, part), BF16),
                pltpu.VMEM(lead + (ring, rows, emb), F32),
                pltpu.VMEM(lead + (ring, rows, emb), BF16),
                pltpu.VMEM(lead + (2, 4, rows, emb), BF16),
                pltpu.VMEM(lead + (2, 4, rows, emb), BF16),
                pltpu.VMEM(lead + (2, 4, rows, emb), BF16),
                pltpu.VMEM((ndp, 2 * emb // 128, 128), F32),
                pltpu.VMEM((ndp, 2 * emb // 128, 128), F32),
                pltpu.SemaphoreType.DMA((5,)),
            ]
            + [pltpu.SemaphoreType.DMA(lead + (2, 4, 2))] * 6
            + [pltpu.SemaphoreType.DMA, pltpu.SemaphoreType.DMA],
            compiler_params=pltpu.CompilerParams(
                collective_id=0, has_side_effects=True, vmem_limit_bytes=56 * 2**20
            ),
            name="vision_block",
        )(live, owners.reshape(1, total // 4), vit_gain, merge_gain, patches, fc1.T, fc2, mid.T, proj)

    return jax.shard_map(
        body,
        mesh=mesh,
        in_specs=(
            P("dp", None), P("dp"), P("dp", None), P(), P(None, "tensor"), P("tensor", None), P(),
            P(None, "tensor"), P("tensor", None),
        ),
        out_specs=P("dp", "tensor"),
        check_vma=False,
    )
```

time: 115 us -> 100 us (0.87)
  local copies, waits for them, and re-layouts: 13.5 us -> 1.47 us
  Pallas kernels: 100 us -> 97.9 us
    unnamed x4 -> x1, local copies, waits for them, and re-layouts: 10.9 us -> 1.47 us
    reshape x2 -> x0, local copies, waits for them, and re-layouts: 2.59 us -> none  [the longest x1 1.3 us: body(): merge_gain.reshape(1, width)]
    pallas_call x1, Pallas kernels: 100 us -> 97.9 us  [body(): pl.pallas_call(kernel, out_shape=jax.ShapeDtypeStruct((2 * ndp, emb), BF1...]
where the time goes in v2:
time: 100 us
  Pallas kernels  97.9 us (98%)
  local copies, waits for them, and re-layouts  1.47 us (1%)
    pallas_call x1, Pallas kernels, body(): pl.pallas_call(kernel, out_shape=jax.ShapeDtypeStruct((2 * ndp, emb), BF1...  97.9 us

profile of v2, /device:TPU:1, one launch (start us, length us, event | category | flops | bytes accessed | tf_op | source)
XLA Modules:
  0.0 100.0 jit_solution(12205608446777172999)
XLA Ops:
  0.7 97.9 %vision_block.1 = bf16[128,256]{1,0:T(8,128)(2,1)} custom-call(s32[1]{0:T(128)S(6)} %copy.11.live_ref, s32[1,128]{1,0:T(1,128)} %bitcast.5, f32[1280]{0:T(1024)} %vit_gain_ref.1, f32[1280]{0:T(1024)} %merge_gain_ref.1, bf16[512,1280]{1,0:T(8,128)(2,1)} %patches_hbm.1, bf16[320,1280]{1,0:T(8,128)(2,1)} %bitcast.4, bf16[320,1280]{1,0:T(8,128)(2,1)} %fc2_hbm.1, ...), custom_call_target="tpu_custom_call" | custom-call | tf_op jit(solution)/shard_map/vision_block/pallas_call | solution.py:296
  98.6 1.5 %copy.12 = bf16[128,256]{1,0:T(8,128)(2,1)} copy(bf16[128,256]{1,0:T(8,128)(2,1)} %vision_block.1) | data formatting | bytes 131072

commit v3 on v2

v3 whole, which is shorter than its diff:
```python
import jax
import jax.numpy as jnp
from jax import lax
from jax.experimental import pallas as pl
from jax.experimental.pallas import tpu as pltpu
from jax.sharding import PartitionSpec as P

MESH = pl.DeviceIdType.MESH
F32 = jnp.float32
BF16 = jnp.bfloat16
STAGES = 2
HALVES = 2
SIGNS = (1, -1)
SUM1 = ((2, 2, 2, 2), (1, 2, 2, 2))
GATHER = ((2, 2, 2, 2), (2, 2, 2, 1))
SUM2 = ((2, 2, 2, 2), (1, 2, 2, 2))
DEPTH = 4


def dot(a, b):
    return jnp.dot(a, b, preferred_element_type=F32)


def dot_t(a, b):
    return lax.dot_general(a, b, (((1,), (1,)), ((), ())), preferred_element_type=F32)


def layer_norm(values, gain):
    mean = jnp.mean(values, axis=-1, keepdims=True)
    centered = values - mean
    variance = jnp.mean(centered * centered, axis=-1, keepdims=True)
    return centered * lax.rsqrt(variance + 1e-06) * gain


def positions(hops):
    left, places = sum(hops), []
    for hop in hops:
        places.append(left)
        left -= hop
    return places


class Reduce:
    def __init__(self, me, ring, sides, own, rounded, relay, got, send_sem, recv_sem):
        self.me, self.ring, self.sides = me, ring, sides
        self.places = [positions(hops) for hops in sides]
        self.own, self.rounded, self.relay = own, rounded, relay
        self.got = got
        self.send_sem, self.recv_sem = send_sem, recv_sem
        self.steps = max(len(hops) for hops in sides)

    def place(self, steps):
        return lax.rem(self.me + (steps + self.ring), self.ring)

    def far(self, d, k):
        source = self.relay.at[d, k] if k else self.rounded.at[self.place(self.places[d][0] * SIGNS[d])]
        return pltpu.make_async_remote_copy(
            src_ref=source, dst_ref=self.got.at[d, k, 0],
            send_sem=self.send_sem, recv_sem=self.recv_sem.at[d, k],
            device_id={"tensor": self.place(self.sides[d][k] * SIGNS[d])}, device_id_type=MESH)

    def has_near(self, d, k):
        return k < len(self.sides[d]) and self.sides[d][k] == 2

    def near(self, d, k):
        return pltpu.make_async_remote_copy(
            src_ref=self.rounded.at[self.place((self.places[d][k] - 1) * SIGNS[d])], dst_ref=self.got.at[d, k, 1],
            send_sem=self.send_sem, recv_sem=self.recv_sem.at[d, k],
            device_id={"tensor": self.place(SIGNS[d])}, device_id_type=MESH)

    def first(self):
        for d in (0, 1):
            self.far(d, 0).start()
        for k in (0, 1):
            for d in (0, 1):
                if self.has_near(d, k):
                    self.near(d, k).start()

    def arrived(self, d, k):
        if not self.has_near(d, k):
            self.far(d, k).wait_recv()
            return self.got[d, k, 0].astype(F32)
        both = self.got.at[d, k]
        pltpu.make_async_copy(both, both, self.recv_sem.at[d, k]).wait()
        return self.got[d, k, 0].astype(F32) + self.got[d, k, 1].astype(F32)

    def step(self, k):
        for d in (0, 1):
            if k < len(self.sides[d]):
                got = self.arrived(d, k - 1)
                mine = self.own[self.place(self.places[d][k] * SIGNS[d])]
                self.relay[d, k] = (mine + got).astype(BF16)
                self.far(d, k).start()
                if self.has_near(d, k + 1):
                    self.near(d, k + 1).start()

    def last(self):
        return self.own[self.me] + self.arrived(0, len(self.sides[0]) - 1) + self.arrived(1, len(self.sides[1]) - 1)

    def drain(self):
        every = self.rounded.at[pl.ds(0, self.ring - 1)]
        pltpu.make_async_copy(every, every, self.send_sem).wait()


class Gather:
    def __init__(self, me, ring, sides, chunks, send_sem, recv_sem, near_sem):
        self.me, self.ring, self.sides, self.chunks = me, ring, sides, chunks
        self.send_sem, self.recv_sem, self.near_sem = send_sem, recv_sem, near_sem
        self.steps = max(len(hops) for hops in sides)

    def place(self, steps):
        return lax.rem(self.me + (steps + self.ring), self.ring)

    def copy(self, d, k, hop, distance):
        chunk = self.chunks.at[self.place(-distance * SIGNS[d])]
        return pltpu.make_async_remote_copy(
            src_ref=chunk, dst_ref=chunk, send_sem=self.send_sem,
            recv_sem=self.near_sem if hop < self.sides[d][k] else self.recv_sem.at[d, k],
            device_id={"tensor": self.place(hop * SIGNS[d])}, device_id_type=MESH)

    def sent(self, d, k, hop):
        return self.copy(d, k, hop, sum(self.sides[d][:k]))

    def landed(self, d, k, hop):
        return self.copy(d, k, hop, sum(self.sides[d][:k]) + hop)

    def step(self, k):
        live = [d for d in (0, 1) if k < len(self.sides[d])]
        for d in live:
            if k > 0:
                self.landed(d, k - 1, self.sides[d][k - 1]).wait_recv()
            self.sent(d, k, self.sides[d][k]).start()
        for d in live:
            if self.sides[d][k] == 2:
                self.sent(d, k, 1).start()

    def last(self):
        for d in (0, 1):
            k = len(self.sides[d]) - 1
            self.landed(d, k, self.sides[d][k]).wait_recv()
        between = self.chunks.at[pl.ds(0, sum(hops.count(2) for hops in self.sides))]
        pltpu.make_async_copy(between, between, self.near_sem).wait()

    def drain(self):
        every = self.chunks.at[pl.ds(0, self.ring - 1)]
        pltpu.make_async_copy(every, every, self.send_sem).wait()


def kernel(
    live_hbm, owner_hbm, vit_gain_hbm, merge_gain_hbm, patches_hbm, fc1_hbm, fc2_hbm, mid_hbm, proj_hbm,
    out_ref,
    live_ref, owner_ref, vit_gain_ref, merge_gain_ref, patches_ref, fc1_ref, fc2_ref, mid_w, proj_w,
    rows, own1, round1, relay1, got1, chunks, own2, round2, relay2, got2,
    outgoing, incoming,
    load_sem, send1, recv1, send_g, recv_g, near_g, send2, recv2, send_x, recv_x,
):
    ring = lax.axis_size("tensor")
    ndp = lax.axis_size("dp")
    me = lax.axis_index("tensor")
    here = lax.axis_index("dp")
    merged = patches_ref.shape[0] // 4
    count = merged // STAGES
    width = patches_ref.shape[1]
    part = width // HALVES
    emb = own2.shape[4]

    barrier = pltpu.get_barrier_semaphore()
    for hops in (1, 2, ring - 2, ring - 1):
        pl.semaphore_signal(barrier, inc=1, device_id={"tensor": lax.rem(me + hops, ring)}, device_id_type=MESH)
    loads = [
        pltpu.make_async_copy(source, target, load_sem.at[i])
        for i, (source, target) in enumerate((
            (patches_hbm, patches_ref), (vit_gain_hbm, vit_gain_ref), (fc1_hbm, fc1_ref), (fc2_hbm, fc2_ref),
            (merge_gain_hbm, merge_gain_ref), (mid_hbm, mid_w), (proj_hbm, proj_w), (owner_hbm, owner_ref), (live_hbm, live_ref)))
    ]
    for load in loads:
        load.start()

    def other(i):
        return lax.rem(here + 1 + lax.rem(i + ndp * 3 // 8, ndp - 1), ndp)

    def greet(i, carry):
        pl.semaphore_signal(barrier, inc=1, device_id={"dp": other(i)}, device_id_type=MESH)
        return carry

    lax.fori_loop(0, ndp - 1, greet, 0)

    def mlp(s):
        total = 4 * count
        to = lax.broadcasted_iota(jnp.int32, (total, total), 0)
        source = lax.broadcasted_iota(jnp.int32, (total, total), 1)
        order = (source == 4 * (to % count) + to // count).astype(BF16)
        ordered = dot(order, patches_ref[s * total : (s + 1) * total, :])
        rows[s] = ordered.astype(BF16).reshape(rows.shape[1:])
        normed = layer_norm(ordered, vit_gain_ref[...].reshape(1, width)).astype(BF16)
        up = dot_t(normed, fc1_ref[...])
        hidden = (up * jax.nn.sigmoid(1.702 * up)).astype(BF16)
        for h in range(HALVES):
            partial = dot(hidden, fc2_ref[:, h * part : (h + 1) * part]).reshape(own1.shape[2:])
            own1[s, h] = partial
            round1[s, h] = partial.astype(BF16)

    stages, halves = range(STAGES), range(HALVES)

    def turned(sides, chain):
        return sides if chain[1] % 2 == 0 else sides[::-1]

    chains = [(s, h) for s in stages for h in halves]
    sums1 = {
        c: Reduce(me, ring, turned(SUM1, c), own1.at[c], round1.at[c], relay1.at[c], got1.at[c], send1.at[c], recv1.at[c])
        for c in chains
    }
    gathers = {c: Gather(me, ring, turned(GATHER, c), chunks.at[c], send_g.at[c], recv_g.at[c], near_g.at[c]) for c in chains}
    sums2 = {
        c: Reduce(me, ring, turned(SUM2, c), own2.at[c], round2.at[c], relay2.at[c], got2.at[c], send2.at[c], recv2.at[c])
        for c in chains
    }

    for load in loads[:5]:
        load.wait()
    for s in stages:
        mlp(s)
        if s == 0:
            pl.semaphore_wait(barrier, 4 + ndp - 1)
        for h in halves:
            sums1[s, h].first()
    for k in range(1, sums1[0, 0].steps):
        for c in chains:
            sums1[c].step(k)
    for s in stages:
        summed = jnp.concatenate([sums1[s, h].last() for h in halves], axis=1)
        vit_out = (rows[s, me].astype(F32) + summed).astype(BF16)
        normed = layer_norm(vit_out.astype(F32), merge_gain_ref[...].reshape(1, width)).astype(BF16)
        for h in halves:
            chunks[s, h, me] = normed[:, h * part : (h + 1) * part]
            gathers[s, h].step(0)
    for k in range(1, gathers[0, 0].steps):
        for c in chains:
            gathers[c].step(k)
    for load in loads[5:]:
        load.wait()
    quarter = ring // 4
    for s in stages:
        turned_mid = jnp.zeros((mid_w.shape[0], count), F32)
        for h in halves:
            gathers[s, h].last()
            for j in range(4):
                block = chunks[s, h, quarter * j : quarter * (j + 1)].reshape(count, part)
                first = j * width + h * part
                turned_mid = turned_mid + dot_t(mid_w[:, first : first + part], block)
        middle = turned_mid.T
        middle = (0.5 * middle * (1.0 + lax.erf(middle * 0.7071067811865476))).astype(BF16)
        for t in range(ring):
            term = dot(middle, proj_w[:, t * emb : (t + 1) * emb])
            for h in halves:
                piece = term[h * (count // HALVES) : (h + 1) * (count // HALVES)]
                own2[s, h, t] = piece
                round2[s, h, t] = piece.astype(BF16)
        for h in halves:
            sums2[s, h].first()
    for k in range(1, sums2[0, 0].steps):
        for c in chains:
            sums2[c].step(k)

    owner = jnp.broadcast_to(owner_ref[...], (merged, merged))
    across = lax.broadcasted_iota(jnp.int32, (merged, merged), 1)
    down = lax.broadcasted_iota(jnp.int32, (merged, merged), 0)
    own_col = owner.astype(F32).T.astype(jnp.int32)
    slot = jnp.sum(jnp.where((owner == own_col) & (down < across), 1.0, 0.0), axis=0, keepdims=True)
    column = lax.broadcasted_iota(jnp.int32, (ndp, merged), 1)
    target = lax.broadcasted_iota(jnp.int32, (ndp, merged), 0)
    kept = (owner[:1] == target) & (column * 4 // (4 * merged // 4) < live_ref[0])
    placing = [jnp.where(kept & (slot == float(k)), 1.0, 0.0).astype(BF16) for k in (0, 1)]

    final = jnp.concatenate([sums2[c].last().astype(BF16) for c in chains], axis=0)
    lanes = outgoing.shape[2]
    for k in (0, 1):
        placed = dot(placing[k], final)
        for h in range(emb // lanes):
            outgoing[:, 2 * k + h, :] = placed[:, h * lanes : (h + 1) * lanes]

    def send(i, carry):
        peer = other(i)
        pltpu.make_async_remote_copy(
            src_ref=outgoing.at[peer], dst_ref=incoming.at[here], send_sem=send_x, recv_sem=recv_x,
            device_id={"dp": peer}, device_id_type=MESH).start()
        return carry

    lax.fori_loop(0, ndp - 1, send, 0)
    incoming[here] = outgoing[here]
    for c in chains:
        sums1[c].drain()
        gathers[c].drain()
        sums2[c].drain()
    others = pl.ds(0, ndp - 1)
    pltpu.make_async_copy(outgoing.at[others], incoming.at[others], send_x).wait()
    pltpu.make_async_copy(outgoing.at[others], incoming.at[others], recv_x).wait()

    row = lax.broadcasted_iota(jnp.int32, (2 * ndp, ndp), 0)
    origin = lax.broadcasted_iota(jnp.int32, (2 * ndp, ndp), 1)
    result = jnp.zeros((2 * ndp, emb), F32)
    for k in (0, 1):
        part = jnp.concatenate([incoming[:, 2 * k + h, :] for h in range(emb // lanes)], axis=1).astype(BF16)
        result = result + dot((row == 2 * origin + k).astype(BF16), part)
    out_ref[...] = result.astype(BF16)


def solution(mesh):
    ring, ndp = mesh.shape["tensor"], mesh.shape["dp"]

    def body(patches, live, owners, vit_gain, fc1, fc2, merge_gain, mid, proj):
        total, width = patches.shape
        chunk = total // STAGES // ring
        count = total // 4 // STAGES
        emb = proj.shape[1] // ring
        part, rows = width // HALVES, count // HALVES
        lead = (STAGES, HALVES)
        return pl.pallas_call(
            kernel,
            out_shape=jax.ShapeDtypeStruct((2 * ndp, emb), BF16),
            in_specs=[pl.BlockSpec(memory_space=pl.ANY)] * 9,
            out_specs=pl.BlockSpec(memory_space=pltpu.VMEM),
            scratch_shapes=[
                pltpu.SMEM((1,), jnp.int32),
                pltpu.VMEM((1, total // 4), jnp.int32),
                pltpu.VMEM((width,), F32),
                pltpu.VMEM((width,), F32),
                pltpu.VMEM(patches.shape, BF16),
                pltpu.VMEM(fc1.shape[::-1], BF16),
                pltpu.VMEM(fc2.shape, BF16),
                pltpu.VMEM(mid.shape[::-1], BF16),
                pltpu.VMEM(proj.shape, BF16),
                pltpu.VMEM((STAGES, ring, chunk, width), BF16),
                pltpu.VMEM(lead + (ring, chunk, part), F32),
                pltpu.VMEM(lead + (ring, chunk, part), BF16),
                pltpu.VMEM(lead + (2, DEPTH, chunk, part), BF16),
                pltpu.VMEM(lead + (2, DEPTH, 2, chunk, part), BF16),
                pltpu.VMEM(lead + (ring, chunk, part), BF16),
                pltpu.VMEM(lead + (ring, rows, emb), F32),
                pltpu.VMEM(lead + (ring, rows, emb), BF16),
                pltpu.VMEM(lead + (2, DEPTH, rows, emb), BF16),
                pltpu.VMEM(lead + (2, DEPTH, 2, rows, emb), BF16),
                pltpu.VMEM((ndp, 2 * emb // 128, 128), F32),
                pltpu.VMEM((ndp, 2 * emb // 128, 128), F32),
                pltpu.SemaphoreType.DMA((9,)),
            ]
            + [pltpu.SemaphoreType.DMA(lead), pltpu.SemaphoreType.DMA(lead + (2, DEPTH))] * 2
            + [pltpu.SemaphoreType.DMA(lead)] * 2
            + [pltpu.SemaphoreType.DMA(lead + (2, DEPTH))]
            + [pltpu.SemaphoreType.DMA, pltpu.SemaphoreType.DMA],
            compiler_params=pltpu.CompilerParams(
                collective_id=0, has_side_effects=True, vmem_limit_bytes=56 * 2**20
            ),
            name="vision_block",
        )(live, owners.reshape(1, total // 4), vit_gain, merge_gain, patches, fc1.T, fc2, mid.T, proj)

    return jax.shard_map(
        body,
        mesh=mesh,
        in_specs=(
            P("dp", None), P("dp"), P("dp", None), P(), P(None, "tensor"), P("tensor", None), P(),
            P(None, "tensor"), P("tensor", None),
        ),
        out_specs=P("dp", "tensor"),
        check_vma=False,
    )
```

time: 100 us -> 96.3 us (0.963)
  Pallas kernels: 97.9 us -> 93.9 us
    pallas_call x1, Pallas kernels: 97.9 us -> 93.9 us  [body(): pl.pallas_call(kernel, out_shape=jax.ShapeDtypeStruct((2 * ndp, emb), BF1...]
where the time goes in v3:
time: 96.3 us; the launch traced here: 96.1 us
  Pallas kernels  93.9 us (98%)
  local copies, waits for them, and re-layouts  1.47 us (2%)
    pallas_call x1, Pallas kernels, body(): pl.pallas_call(kernel, out_shape=jax.ShapeDtypeStruct((2 * ndp, emb), BF1...  93.9 us

profile of v3, /device:TPU:1, one launch (start us, length us, event | category | flops | bytes accessed | tf_op | source)
XLA Modules:
  0.0 96.1 jit_solution(12493681790102963482)
XLA Ops:
  0.7 93.9 %vision_block.1 = bf16[128,256]{1,0:T(8,128)(2,1)} custom-call(s32[1]{0:T(128)S(6)} %copy.11.live_hbm, s32[1,128]{1,0:T(1,128)} %bitcast.5, f32[1280]{0:T(1024)} %vit_gain_hbm.1, f32[1280]{0:T(1024)} %merge_gain_hbm.1, bf16[512,1280]{1,0:T(8,128)(2,1)} %patches_hbm.1, bf16[320,1280]{1,0:T(8,128)(2,1)} %bitcast.4, bf16[320,1280]{1,0:T(8,128)(2,1)} %fc2_hbm.1, ...), custom_call_target="tpu_custom_call" | custom-call | tf_op jit(solution)/shard_map/vision_block/pallas_call | solution.py:318
  94.6 1.5 %copy.12 = bf16[128,256]{1,0:T(8,128)(2,1)} copy(bf16[128,256]{1,0:T(8,128)(2,1)} %vision_block.1) | data formatting | bytes 131072

commit v4 on v3

--- a/solution.py
+++ b/solution.py
@@ -1,3 +1,5 @@
+import functools
+
 import jax
 import jax.numpy as jnp
 from jax import lax
@@ -15,6 +17,7 @@
 GATHER = ((2, 2, 2, 2), (2, 2, 2, 1))
 SUM2 = ((2, 2, 2, 2), (1, 2, 2, 2))
 DEPTH = 4
+LAG = 0
 
 
 def dot(a, b):
@@ -167,13 +170,16 @@
     barrier = pltpu.get_barrier_semaphore()
     for hops in (1, 2, ring - 2, ring - 1):
         pl.semaphore_signal(barrier, inc=1, device_id={"tensor": lax.rem(me + hops, ring)}, device_id_type=MESH)
+    half = patches_ref.shape[0] // STAGES
     loads = [
         pltpu.make_async_copy(source, target, load_sem.at[i])
         for i, (source, target) in enumerate((
-            (patches_hbm, patches_ref), (vit_gain_hbm, vit_gain_ref), (fc1_hbm, fc1_ref), (fc2_hbm, fc2_ref),
-            (merge_gain_hbm, merge_gain_ref), (mid_hbm, mid_w), (proj_hbm, proj_w), (owner_hbm, owner_ref), (live_hbm, live_ref)))
+            (patches_hbm.at[pl.ds(0, half)], patches_ref.at[pl.ds(0, half)]), (vit_gain_hbm, vit_gain_ref),
+            (fc1_hbm, fc1_ref), (fc2_hbm, fc2_ref),
+            (patches_hbm.at[pl.ds(half, half)], patches_ref.at[pl.ds(half, half)]), (merge_gain_hbm, merge_gain_ref),
+            (mid_hbm, mid_w), (proj_hbm, proj_w), (owner_hbm, owner_ref), (live_hbm, live_ref)))
     ]
-    for load in loads:
+    for load in loads[:4]:
         load.start()
 
     def other(i):
@@ -216,31 +222,34 @@
         for c in chains
     }
 
-    for load in loads[:5]:
+    for load in loads[:4]:
         load.wait()
-    for s in stages:
+    for load in loads[4:]:
+        load.start()
+
+    def start_sum1(s):
+        if s == 1:
+            for load in loads[4:6]:
+                load.wait()
         mlp(s)
         if s == 0:
             pl.semaphore_wait(barrier, 4 + ndp - 1)
         for h in halves:
             sums1[s, h].first()
-    for k in range(1, sums1[0, 0].steps):
-        for c in chains:
-            sums1[c].step(k)
-    for s in stages:
+
+    def start_gather(s):
         summed = jnp.concatenate([sums1[s, h].last() for h in halves], axis=1)
         vit_out = (rows[s, me].astype(F32) + summed).astype(BF16)
         normed = layer_norm(vit_out.astype(F32), merge_gain_ref[...].reshape(1, width)).astype(BF16)
         for h in halves:
             chunks[s, h, me] = normed[:, h * part : (h + 1) * part]
             gathers[s, h].step(0)
-    for k in range(1, gathers[0, 0].steps):
-        for c in chains:
-            gathers[c].step(k)
-    for load in loads[5:]:
-        load.wait()
-    quarter = ring // 4
-    for s in stages:
+
+    def start_sum2(s):
+        if s == 0:
+            for load in loads[6:]:
+                load.wait()
+        quarter = ring // 4
         turned_mid = jnp.zeros((mid_w.shape[0], count), F32)
         for h in halves:
             gathers[s, h].last()
@@ -258,9 +267,24 @@
                 round2[s, h, t] = piece.astype(BF16)
         for h in halves:
             sums2[s, h].first()
-    for k in range(1, sums2[0, 0].steps):
-        for c in chains:
-            sums2[c].step(k)
+
+    def steps_of(group, s):
+        def advance(k):
+            for h in halves:
+                group[s, h].step(k)
+
+        return [functools.partial(advance, k) for k in range(1, group[s, 0].steps)]
+
+    events = [
+        [functools.partial(start_sum1, s)] + steps_of(sums1, s)
+        + [functools.partial(start_gather, s)] + steps_of(gathers, s)
+        + [functools.partial(start_sum2, s)] + steps_of(sums2, s)
+        for s in stages
+    ]
+    for turn in range(len(events[0]) + LAG * (STAGES - 1)):
+        for s in stages:
+            if 0 <= turn - LAG * s < len(events[s]):
+                events[s][turn - LAG * s]()
 
     owner = jnp.broadcast_to(owner_ref[...], (merged, merged))
     across = lax.broadcasted_iota(jnp.int32, (merged, merged), 1)
@@ -277,7 +301,7 @@
     for k in (0, 1):
         placed = dot(placing[k], final)
         for h in range(emb // lanes):
-            outgoing[:, 2 * k + h, :] = placed[:, h * lanes : (h + 1) * lanes]
+            outgoing[:, 2 * k + h, :] = placed[:, h * lanes : (h + 1) * lanes].astype(BF16)
 
     def send(i, carry):
         peer = other(i)
@@ -300,7 +324,7 @@
     origin = lax.broadcasted_iota(jnp.int32, (2 * ndp, ndp), 1)
     result = jnp.zeros((2 * ndp, emb), F32)
     for k in (0, 1):
-        part = jnp.concatenate([incoming[:, 2 * k + h, :] for h in range(emb // lanes)], axis=1).astype(BF16)
+        part = jnp.concatenate([incoming[:, 2 * k + h, :] for h in range(emb // lanes)], axis=1)
         result = result + dot((row == 2 * origin + k).astype(BF16), part)
     out_ref[...] = result.astype(BF16)
 
@@ -340,9 +364,9 @@
                 pltpu.VMEM(lead + (ring, rows, emb), BF16),
                 pltpu.VMEM(lead + (2, DEPTH, rows, emb), BF16),
                 pltpu.VMEM(lead + (2, DEPTH, 2, rows, emb), BF16),
-                pltpu.VMEM((ndp, 2 * emb // 128, 128), F32),
-                pltpu.VMEM((ndp, 2 * emb // 128, 128), F32),
-                pltpu.SemaphoreType.DMA((9,)),
+                pltpu.VMEM((ndp, 2 * emb // 128, 128), BF16),
+                pltpu.VMEM((ndp, 2 * emb // 128, 128), BF16),
+                pltpu.SemaphoreType.DMA((10,)),
             ]
             + [pltpu.SemaphoreType.DMA(lead), pltpu.SemaphoreType.DMA(lead + (2, DEPTH))] * 2
             + [pltpu.SemaphoreType.DMA(lead)] * 2

time: 96.3 us -> 96.2 us (level)
  no operation moved by 1% of the time
where the time goes in v4:
time: 96.2 us; the launch traced here: 96 us
  Pallas kernels  93.9 us (98%)
  local copies, waits for them, and re-layouts  1.47 us (2%)
    pallas_call x1, Pallas kernels, body(): pl.pallas_call(kernel, out_shape=jax.ShapeDtypeStruct((2 * ndp, emb), BF1...  93.9 us

profile of v4, /device:TPU:1, one launch (start us, length us, event | category | flops | bytes accessed | tf_op | source)
XLA Modules:
  0.0 96.0 jit_solution(13259029437790492002)
XLA Ops:
  0.7 93.9 %vision_block.1 = bf16[128,256]{1,0:T(8,128)(2,1)} custom-call(s32[1]{0:T(128)S(6)} %copy.11.live_hbm, s32[1,128]{1,0:T(1,128)} %bitcast.5, f32[1280]{0:T(1024)} %vit_gain_hbm.1, f32[1280]{0:T(1024)} %merge_gain_hbm.1, bf16[512,1280]{1,0:T(8,128)(2,1)} %patches_hbm.1, bf16[320,1280]{1,0:T(8,128)(2,1)} %bitcast.4, bf16[320,1280]{1,0:T(8,128)(2,1)} %fc2_hbm.1, ...), custom_call_target="tpu_custom_call" | custom-call | tf_op jit(solution)/shard_map/vision_block/pallas_call | solution.py:342
  94.5 1.5 %copy.12 = bf16[128,256]{1,0:T(8,128)(2,1)} copy(bf16[128,256]{1,0:T(8,128)(2,1)} %vision_block.1) | data formatting | bytes 131072

commit v5 on v4

--- a/solution.py
+++ b/solution.py
@@ -301,7 +301,7 @@
     for k in (0, 1):
         placed = dot(placing[k], final)
         for h in range(emb // lanes):
-            outgoing[:, 2 * k + h, :] = placed[:, h * lanes : (h + 1) * lanes].astype(BF16)
+            outgoing[:, 2 * k + h, :] = placed[:, h * lanes : (h + 1) * lanes]
 
     def send(i, carry):
         peer = other(i)
@@ -324,7 +324,7 @@
     origin = lax.broadcasted_iota(jnp.int32, (2 * ndp, ndp), 1)
     result = jnp.zeros((2 * ndp, emb), F32)
     for k in (0, 1):
-        part = jnp.concatenate([incoming[:, 2 * k + h, :] for h in range(emb // lanes)], axis=1)
+        part = jnp.concatenate([incoming[:, 2 * k + h, :] for h in range(emb // lanes)], axis=1).astype(BF16)
         result = result + dot((row == 2 * origin + k).astype(BF16), part)
     out_ref[...] = result.astype(BF16)
 
@@ -364,8 +364,8 @@
                 pltpu.VMEM(lead + (ring, rows, emb), BF16),
                 pltpu.VMEM(lead + (2, DEPTH, rows, emb), BF16),
                 pltpu.VMEM(lead + (2, DEPTH, 2, rows, emb), BF16),
-                pltpu.VMEM((ndp, 2 * emb // 128, 128), BF16),
-                pltpu.VMEM((ndp, 2 * emb // 128, 128), BF16),
+                pltpu.VMEM((ndp, 2 * emb // 128, 128), F32),
+                pltpu.VMEM((ndp, 2 * emb // 128, 128), F32),
                 pltpu.SemaphoreType.DMA((10,)),
             ]
             + [pltpu.SemaphoreType.DMA(lead), pltpu.SemaphoreType.DMA(lead + (2, DEPTH))] * 2

time: 96.2 us -> 96.5 us (level)
  no operation moved by 1% of the time
where the time goes in v5:
time: 96.5 us; the launch traced here: 96.2 us
  Pallas kernels  94.1 us (98%)
  local copies, waits for them, and re-layouts  1.47 us (2%)
    pallas_call x1, Pallas kernels, body(): pl.pallas_call(kernel, out_shape=jax.ShapeDtypeStruct((2 * ndp, emb), BF1...  94.1 us

profile of v5, /device:TPU:1, one launch (start us, length us, event | category | flops | bytes accessed | tf_op | source)
XLA Modules:
  0.0 96.2 jit_solution(16741340377381503083)
XLA Ops:
  0.7 94.1 %vision_block.1 = bf16[128,256]{1,0:T(8,128)(2,1)} custom-call(s32[1]{0:T(128)S(6)} %copy.11.live_hbm, s32[1,128]{1,0:T(1,128)} %bitcast.5, f32[1280]{0:T(1024)} %vit_gain_hbm.1, f32[1280]{0:T(1024)} %merge_gain_hbm.1, bf16[512,1280]{1,0:T(8,128)(2,1)} %patches_hbm.1, bf16[320,1280]{1,0:T(8,128)(2,1)} %bitcast.4, bf16[320,1280]{1,0:T(8,128)(2,1)} %fc2_hbm.1, ...), custom_call_target="tpu_custom_call" | custom-call | tf_op jit(solution)/shard_map/vision_block/pallas_call | solution.py:342
  94.8 1.5 %copy.12 = bf16[128,256]{1,0:T(8,128)(2,1)} copy(bf16[128,256]{1,0:T(8,128)(2,1)} %vision_block.1) | data formatting | bytes 131072

commit v6 on v5

--- a/solution.py
+++ b/solution.py
@@ -58,17 +58,20 @@
     def far(self, d, k):
         source = self.relay.at[d, k] if k else self.rounded.at[self.place(self.places[d][0] * SIGNS[d])]
         return pltpu.make_async_remote_copy(
-            src_ref=source, dst_ref=self.got.at[d, k, 0],
-            send_sem=self.send_sem, recv_sem=self.recv_sem.at[d, k],
+            src_ref=source, dst_ref=self.got.at[k, d],
+            send_sem=self.send_sem, recv_sem=self.recv_sem.at[k],
             device_id={"tensor": self.place(self.sides[d][k] * SIGNS[d])}, device_id_type=MESH)
 
     def has_near(self, d, k):
         return k < len(self.sides[d]) and self.sides[d][k] == 2
 
+    def near_slot(self, d, k):
+        return 2 + sum(self.has_near(other, k) for other in range(d))
+
     def near(self, d, k):
         return pltpu.make_async_remote_copy(
-            src_ref=self.rounded.at[self.place((self.places[d][k] - 1) * SIGNS[d])], dst_ref=self.got.at[d, k, 1],
-            send_sem=self.send_sem, recv_sem=self.recv_sem.at[d, k],
+            src_ref=self.rounded.at[self.place((self.places[d][k] - 1) * SIGNS[d])], dst_ref=self.got.at[k, self.near_slot(d, k)],
+            send_sem=self.send_sem, recv_sem=self.recv_sem.at[k],
             device_id={"tensor": self.place(SIGNS[d])}, device_id_type=MESH)
 
     def first(self):
@@ -79,26 +82,29 @@
                 if self.has_near(d, k):
                     self.near(d, k).start()
 
-    def arrived(self, d, k):
-        if not self.has_near(d, k):
-            self.far(d, k).wait_recv()
-            return self.got[d, k, 0].astype(F32)
-        both = self.got.at[d, k]
-        pltpu.make_async_copy(both, both, self.recv_sem.at[d, k]).wait()
-        return self.got[d, k, 0].astype(F32) + self.got[d, k, 1].astype(F32)
+    def arrived(self, k):
+        together = self.got.at[k, pl.ds(0, 2 + sum(self.has_near(d, k) for d in (0, 1)))]
+        pltpu.make_async_copy(together, together, self.recv_sem.at[k]).wait()
+        totals = []
+        for d in (0, 1):
+            total = self.got[k, d].astype(F32)
+            if self.has_near(d, k):
+                total = total + self.got[k, self.near_slot(d, k)].astype(F32)
+            totals.append(total)
+        return totals
 
     def step(self, k):
-        for d in (0, 1):
-            if k < len(self.sides[d]):
-                got = self.arrived(d, k - 1)
-                mine = self.own[self.place(self.places[d][k] * SIGNS[d])]
-                self.relay[d, k] = (mine + got).astype(BF16)
-                self.far(d, k).start()
-                if self.has_near(d, k + 1):
-                    self.near(d, k + 1).start()
+        got = self.arrived(k - 1)
+        for d in (0, 1):
+            mine = self.own[self.place(self.places[d][k] * SIGNS[d])]
+            self.relay[d, k] = (mine + got[d]).astype(BF16)
+            self.far(d, k).start()
+            if self.has_near(d, k + 1):
+                self.near(d, k + 1).start()
 
     def last(self):
-        return self.own[self.me] + self.arrived(0, len(self.sides[0]) - 1) + self.arrived(1, len(self.sides[1]) - 1)
+        one, other = self.arrived(self.steps - 1)
+        return self.own[self.me] + one + other
 
     def drain(self):
         every = self.rounded.at[pl.ds(0, self.ring - 1)]
@@ -118,29 +124,26 @@
         chunk = self.chunks.at[self.place(-distance * SIGNS[d])]
         return pltpu.make_async_remote_copy(
             src_ref=chunk, dst_ref=chunk, send_sem=self.send_sem,
-            recv_sem=self.near_sem if hop < self.sides[d][k] else self.recv_sem.at[d, k],
+            recv_sem=self.near_sem if hop < self.sides[d][k] else self.recv_sem.at[k],
             device_id={"tensor": self.place(hop * SIGNS[d])}, device_id_type=MESH)
 
     def sent(self, d, k, hop):
         return self.copy(d, k, hop, sum(self.sides[d][:k]))
 
-    def landed(self, d, k, hop):
-        return self.copy(d, k, hop, sum(self.sides[d][:k]) + hop)
+    def landed(self):
+        return self.chunks.at[pl.ds(0, 2)]
 
     def step(self, k):
-        live = [d for d in (0, 1) if k < len(self.sides[d])]
-        for d in live:
-            if k > 0:
-                self.landed(d, k - 1, self.sides[d][k - 1]).wait_recv()
+        if k > 0:
+            pltpu.make_async_copy(self.landed(), self.landed(), self.recv_sem.at[k - 1]).wait()
+        for d in (0, 1):
             self.sent(d, k, self.sides[d][k]).start()
-        for d in live:
+        for d in (0, 1):
             if self.sides[d][k] == 2:
                 self.sent(d, k, 1).start()
 
     def last(self):
-        for d in (0, 1):
-            k = len(self.sides[d]) - 1
-            self.landed(d, k, self.sides[d][k]).wait_recv()
+        pltpu.make_async_copy(self.landed(), self.landed(), self.recv_sem.at[self.steps - 1]).wait()
         between = self.chunks.at[pl.ds(0, sum(hops.count(2) for hops in self.sides))]
         pltpu.make_async_copy(between, between, self.near_sem).wait()
 
@@ -358,19 +361,19 @@
                 pltpu.VMEM(lead + (ring, chunk, part), F32),
                 pltpu.VMEM(lead + (ring, chunk, part), BF16),
                 pltpu.VMEM(lead + (2, DEPTH, chunk, part), BF16),
-                pltpu.VMEM(lead + (2, DEPTH, 2, chunk, part), BF16),
+                pltpu.VMEM(lead + (DEPTH, 4, chunk, part), BF16),
                 pltpu.VMEM(lead + (ring, chunk, part), BF16),
                 pltpu.VMEM(lead + (ring, rows, emb), F32),
                 pltpu.VMEM(lead + (ring, rows, emb), BF16),
                 pltpu.VMEM(lead + (2, DEPTH, rows, emb), BF16),
-                pltpu.VMEM(lead + (2, DEPTH, 2, rows, emb), BF16),
+                pltpu.VMEM(lead + (DEPTH, 4, rows, emb), BF16),
                 pltpu.VMEM((ndp, 2 * emb // 128, 128), F32),
                 pltpu.VMEM((ndp, 2 * emb // 128, 128), F32),
                 pltpu.SemaphoreType.DMA((10,)),
             ]
-            + [pltpu.SemaphoreType.DMA(lead), pltpu.SemaphoreType.DMA(lead + (2, DEPTH))] * 2
+            + [pltpu.SemaphoreType.DMA(lead), pltpu.SemaphoreType.DMA(lead + (DEPTH,))] * 2
             + [pltpu.SemaphoreType.DMA(lead)] * 2
-            + [pltpu.SemaphoreType.DMA(lead + (2, DEPTH))]
+            + [pltpu.SemaphoreType.DMA(lead + (DEPTH,))]
             + [pltpu.SemaphoreType.DMA, pltpu.SemaphoreType.DMA],
             compiler_params=pltpu.CompilerParams(
                 collective_id=0, has_side_effects=True, vmem_limit_bytes=56 * 2**20

time: 96.5 us -> 96.5 us (level)
  no operation moved by 1% of the time
where the time goes in v6:
time: 96.5 us; the launch traced here: 96.3 us
  Pallas kernels  94.2 us (98%)
  local copies, waits for them, and re-layouts  1.47 us (2%)
    pallas_call x1, Pallas kernels, body(): pl.pallas_call(kernel, out_shape=jax.ShapeDtypeStruct((2 * ndp, emb), BF1...  94.2 us

profile of v6, /device:TPU:1, one launch (start us, length us, event | category | flops | bytes accessed | tf_op | source)
XLA Modules:
  0.0 96.3 jit_solution(2722479721235639597)
XLA Ops:
  0.7 94.2 %vision_block.1 = bf16[128,256]{1,0:T(8,128)(2,1)} custom-call(s32[1]{0:T(128)S(6)} %copy.11.live_hbm, s32[1,128]{1,0:T(1,128)} %bitcast.5, f32[1280]{0:T(1024)} %vit_gain_hbm.1, f32[1280]{0:T(1024)} %merge_gain_hbm.1, bf16[512,1280]{1,0:T(8,128)(2,1)} %patches_hbm.1, bf16[320,1280]{1,0:T(8,128)(2,1)} %bitcast.4, bf16[320,1280]{1,0:T(8,128)(2,1)} %fc2_hbm.1, ...), custom_call_target="tpu_custom_call" | custom-call | tf_op jit(solution)/shard_map/vision_block/pallas_call | solution.py:345
  94.8 1.5 %copy.12 = bf16[128,256]{1,0:T(8,128)(2,1)} copy(bf16[128,256]{1,0:T(8,128)(2,1)} %vision_block.1) | data formatting | bytes 131072
